TPU v7x, 128 devices: a whole 4x4x4 slice. The times are simulated.
128 devices in a mesh: dp: 4 (over y_hi, core), seq: 32 (over y_lo, x, z).
Axes of the slice: x: 4, y: 4 (y_hi: 2, y_lo: 2; y = y_hi * 2 + y_lo), z: 4, core: 2. Of those that a mesh axis runs over, the one named last changes fastest.
Arguments:
- tokens: bfloat16 [4, 4096, 1024], P('dp', 'seq'), may hold values from -6 to 6
- out_grad: bfloat16 [4, 4096, 1024], P('dp', 'seq'), may hold values from -6 to 6
- piece_starts: int32 [4, 6], P('dp'), may hold values from 0 to 3840, as said below
- span_order: int32 [4, 64], P('dp'), may hold values from 0 to 63, each once within a row
- ln1_gain: bfloat16 [1, 1024], P(None, ('dp', 'seq')), may hold values from 0.5 to 1.5
- ln1_bias: bfloat16 [1, 1024], P(None, ('dp', 'seq')), may hold values from -4 to 4
- qkv_weight: bfloat16 [1, 1024, 3072], P(None, ('dp', 'seq')), may hold values from -0.1875 to 0.1875
- query_bias: bfloat16 [1, 1024], P(None, ('dp', 'seq')), may hold values from -4 to 4
- value_bias: bfloat16 [1, 1024], P(None, ('dp', 'seq')), may hold values from -4 to 4
- out_weight: bfloat16 [1, 1024, 1024], P(None, ('dp', 'seq')), may hold values from -2 to 2
- out_bias: bfloat16 [1, 1024], P(None, ('dp', 'seq')), may hold values from -3 to 3
- ln2_gain: bfloat16 [1, 1024], P(None, ('dp', 'seq')), may hold values from 0.5 to 1.5
- ln2_bias: bfloat16 [1, 1024], P(None, ('dp', 'seq')), may hold values from -4 to 4
- fc_weight: bfloat16 [1, 1024, 4096], P(None, ('dp', 'seq')), may hold values from -0.1875 to 0.1875
- fc_bias: bfloat16 [1, 4096], P(None, ('dp', 'seq')), may hold values from -4 to 4
- proj_weight: bfloat16 [1, 4096, 1024], P(None, ('dp', 'seq')), may hold values from -0.09375 to 0.09375
- proj_bias: bfloat16 [1, 1024], P(None, ('dp', 'seq')), may hold values from -3 to 3
Outputs:
- out: bfloat16 [4, 4096, 1024], P('dp', 'seq')
- grad_tokens: float32 [4, 4096, 1024], P('dp', 'seq')
- grad_ln1_gain: float32 [1, 1024], P(None, ('dp', 'seq'))
- grad_ln1_bias: float32 [1, 1024], P(None, ('dp', 'seq'))
- grad_qkv_weight: float32 [1, 1024, 3072], P(None, ('dp', 'seq'))
- grad_query_bias: float32 [1, 1024], P(None, ('dp', 'seq'))
- grad_value_bias: float32 [1, 1024], P(None, ('dp', 'seq'))
- grad_out_weight: float32 [1, 1024, 1024], P(None, ('dp', 'seq'))
- grad_out_bias: float32 [1, 1024], P(None, ('dp', 'seq'))
- grad_ln2_gain: float32 [1, 1024], P(None, ('dp', 'seq'))
- grad_ln2_bias: float32 [1, 1024], P(None, ('dp', 'seq'))
- grad_fc_weight: float32 [1, 1024, 4096], P(None, ('dp', 'seq'))
- grad_fc_bias: float32 [1, 4096], P(None, ('dp', 'seq'))
- grad_proj_weight: float32 [1, 4096, 1024], P(None, ('dp', 'seq'))
- grad_proj_bias: float32 [1, 1024], P(None, ('dp', 'seq'))
Inputs may be any that keep to these rules, and one draw needn't show every extreme that they name: `piece_starts`: in each row the starts rise, and each start is at least 256 after the one before, so pieces never intersect. `span_order`: each row names every block 0 to 63 exactly once.
All inputs are finite; a program needn't handle non-finite values.
Results may differ from a plain program's by a relative error of at most 0.0158.
Values may be sent and summed in bfloat16 or wider, within the bound.
No kernel may reach another device: no remote copies, remote signals or barrier semaphores. Data moves between devices by JAX's collectives and lax.ppermute only.
A program may use at most 192 MiB of HBM per device.

v0:
```python
import jax
import jax.numpy as jnp
from jax import lax
from jax.sharding import PartitionSpec as P

D = 1024
HEAD_DIM = 64
LAYERS = 1
PIECE = 256


EPS = 1e-05
NEG = -1e30


def layer_norm(values, gain, shift):
    center = values - jnp.mean(values, axis=-1, keepdims=True)
    spread = jnp.mean(center * center, axis=-1, keepdims=True)
    return center * lax.rsqrt(spread + EPS) * gain + shift


def gelu_tanh(values):
    return (
        0.5
        * values
        * (1.0 + jnp.tanh(0.7978845608028654 * (values + 0.044715 * values * values * values)))
    )


def plain_product(left_side, right_side):
    return jnp.dot(left_side, right_side, preferred_element_type=jnp.float32)


def left_product(left_side, right_side):
    return lax.dot_general(
        left_side, right_side, (((0,), (0,)), ((), ())), preferred_element_type=jnp.float32
    )


def right_product(left_side, right_side):
    return lax.dot_general(
        left_side, right_side, (((1,), (1,)), ((), ())), preferred_element_type=jnp.float32
    )


def column_sum(values):
    return jnp.sum(values.astype(jnp.float32), axis=0)


def piece_number(positions, starts):
    inside = (positions[:, None] >= starts[None, :]) & (
        positions[:, None] < starts[None, :] + PIECE
    )
    labels = jnp.arange(starts.shape[0], dtype=jnp.int32)[None, :] + 1
    return jnp.sum(jnp.where(inside, labels, 0), axis=1)


def pair_view(values, pair_index):
    row_count = values.shape[0]
    pair_count = values.shape[1] // (2 * HEAD_DIM)
    pair_block = lax.dynamic_index_in_dim(
        values.reshape(row_count, pair_count, 2 * HEAD_DIM), pair_index, 1, keepdims=False
    )
    return pair_block.reshape(row_count, 2, HEAD_DIM)


def pair_scores(query_pair, key_pair, allowed):
    scores = jnp.einsum(
        "rhd,khd->hrk", query_pair, key_pair, preferred_element_type=jnp.float32
    ) * HEAD_DIM ** (-0.5)
    return jnp.where(allowed[None], scores, NEG)


def attend_forward(queries, keys_all, values_all, allowed):
    pair_count = queries.shape[1] // (2 * HEAD_DIM)

    def one_pair(pair_index):
        query_pair = pair_view(queries, pair_index)
        key_pair = pair_view(keys_all, pair_index)
        value_pair = pair_view(values_all, pair_index)
        scores = pair_scores(query_pair, key_pair, allowed)
        maxima = jnp.max(scores, axis=-1, keepdims=True)
        raised = jnp.exp(scores - maxima)
        totals = jnp.sum(raised, axis=-1, keepdims=True)
        attn_weights = (raised / totals).astype(jnp.bfloat16)
        mixture = jnp.einsum(
            "hrk,khd->rhd", attn_weights, value_pair, preferred_element_type=jnp.float32
        )
        return (mixture.reshape(mixture.shape[0], 2 * HEAD_DIM), (maxima + jnp.log(totals))[..., 0])

    return lax.map(one_pair, jnp.arange(pair_count))


def attend_backward(queries, keys_all, values_all, allowed, log_totals, grad_attended):
    pair_count = queries.shape[1] // (2 * HEAD_DIM)
    score_scale = HEAD_DIM ** (-0.5)

    def one_pair(pair_index):
        query_pair = pair_view(queries, pair_index)
        key_pair = pair_view(keys_all, pair_index)
        value_pair = pair_view(values_all, pair_index)
        grad_pair = pair_view(grad_attended, pair_index)
        scores = pair_scores(query_pair, key_pair, allowed)
        pair_totals = lax.dynamic_index_in_dim(log_totals, pair_index, 0, keepdims=False)
        attn_weights = jnp.exp(scores - pair_totals[..., None])
        grad_weights = jnp.einsum(
            "rhd,khd->hrk", grad_pair, value_pair, preferred_element_type=jnp.float32
        )
        delta = jnp.sum(attn_weights * grad_weights, axis=-1, keepdims=True)
        grad_scores = (attn_weights * (grad_weights - delta)).astype(jnp.bfloat16)
        grad_query = (
            jnp.einsum("hrk,khd->rhd", grad_scores, key_pair, preferred_element_type=jnp.float32)
            * score_scale
        )
        grad_key = (
            jnp.einsum("hrk,rhd->khd", grad_scores, query_pair, preferred_element_type=jnp.float32)
            * score_scale
        )
        grad_value = jnp.einsum(
            "hrk,rhd->khd",
            attn_weights.astype(jnp.bfloat16),
            grad_pair,
            preferred_element_type=jnp.float32,
        )
        return (
            grad_query.reshape(grad_query.shape[0], 2 * HEAD_DIM),
            grad_key.reshape(grad_key.shape[0], 2 * HEAD_DIM),
            grad_value.reshape(grad_value.shape[0], 2 * HEAD_DIM),
        )

    return lax.map(one_pair, jnp.arange(pair_count))


def side_by_side(values, row_count):
    return values.transpose(1, 0, 2).reshape(row_count, values.shape[0] * values.shape[2])


def on_device(
    tokens,
    out_grad,
    piece_starts,
    span_order,
    ln1_gain,
    ln1_bias,
    qkv_weight,
    query_bias,
    value_bias,
    out_weight,
    out_bias,
    ln2_gain,
    ln2_bias,
    fc_weight,
    fc_bias,
    proj_weight,
    proj_bias,
):
    row_count = tokens.shape[1]
    span_rows = row_count // 2
    seq_index = lax.axis_index("seq")
    block_order = span_order[0]
    key_pos = (
        block_order[:, None] * span_rows + jnp.arange(span_rows, dtype=jnp.int32)[None, :]
    ).reshape(-1)
    query_pos = lax.dynamic_slice_in_dim(key_pos, seq_index * row_count, row_count)
    starts = piece_starts[0]
    piece_key = piece_number(key_pos, starts)
    piece_query = piece_number(query_pos, starts)
    allowed = (key_pos[None, :] <= query_pos[:, None]) | (
        piece_query[:, None] == piece_key[None, :]
    ) & (piece_query[:, None] > 0)

    def rows_of(values, part):
        return values[part * span_rows : (part + 1) * span_rows]

    hidden = tokens[0].astype(jnp.float32)
    layer_index = 0
    normed_list = []
    query_list = []
    key_list = []
    value_list = []
    for part in range(2):
        first_gain = lax.all_gather(ln1_gain[layer_index], ("dp", "seq"), axis=0, tiled=True)
        first_shift = lax.all_gather(ln1_bias[layer_index], ("dp", "seq"), axis=0, tiled=True)
        qkv_matrix = lax.all_gather(qkv_weight[layer_index], ("dp", "seq"), axis=0, tiled=True)
        query_shift = lax.all_gather(query_bias[layer_index], ("dp", "seq"), axis=0, tiled=True)
        value_shift = lax.all_gather(value_bias[layer_index], ("dp", "seq"), axis=0, tiled=True)
        normed_part = layer_norm(
            rows_of(hidden, part), first_gain.astype(jnp.float32), first_shift.astype(jnp.float32)
        ).astype(jnp.bfloat16)
        projected = plain_product(normed_part, qkv_matrix)
        normed_list.append(normed_part)
        query_list.append((projected[:, :D] + query_shift.astype(jnp.float32)).astype(jnp.bfloat16))
        key_list.append(projected[:, D : 2 * D].astype(jnp.bfloat16))
        value_list.append(
            (projected[:, 2 * D :] + value_shift.astype(jnp.float32)).astype(jnp.bfloat16)
        )
    normed = jnp.concatenate(normed_list, axis=0)
    queries = jnp.concatenate(query_list, axis=0)
    keys_mine = jnp.concatenate(key_list, axis=0)
    values_mine = jnp.concatenate(value_list, axis=0)
    keys_all = lax.all_gather(keys_mine, "seq", axis=0, tiled=True)
    values_all = lax.all_gather(values_mine, "seq", axis=0, tiled=True)
    mixture, log_totals = attend_forward(queries, keys_all, values_all, allowed)
    attended = side_by_side(mixture, row_count).astype(jnp.bfloat16)
    middle_list = []
    normed_two_list = []
    pre_list = []
    act_list = []
    next_list = []
    for part in range(2):
        out_matrix = lax.all_gather(out_weight[layer_index], ("dp", "seq"), axis=0, tiled=True)
        out_shift = lax.all_gather(out_bias[layer_index], ("dp", "seq"), axis=0, tiled=True)
        second_gain = lax.all_gather(ln2_gain[layer_index], ("dp", "seq"), axis=0, tiled=True)
        second_shift = lax.all_gather(ln2_bias[layer_index], ("dp", "seq"), axis=0, tiled=True)
        fc_matrix = lax.all_gather(fc_weight[layer_index], ("dp", "seq"), axis=0, tiled=True)
        fc_shift = lax.all_gather(fc_bias[layer_index], ("dp", "seq"), axis=0, tiled=True)
        proj_matrix = lax.all_gather(proj_weight[layer_index], ("dp", "seq"), axis=0, tiled=True)
        proj_shift = lax.all_gather(proj_bias[layer_index], ("dp", "seq"), axis=0, tiled=True)
        middle_part = (
            rows_of(hidden, part)
            + plain_product(rows_of(attended, part), out_matrix)
            + out_shift.astype(jnp.float32)
        )
        normed_two_part = layer_norm(
            middle_part, second_gain.astype(jnp.float32), second_shift.astype(jnp.float32)
        ).astype(jnp.bfloat16)
        pre_part = plain_product(normed_two_part, fc_matrix) + fc_shift.astype(jnp.float32)
        act_part = gelu_tanh(pre_part).astype(jnp.bfloat16)
        next_part = (
            middle_part + plain_product(act_part, proj_matrix) + proj_shift.astype(jnp.float32)
        )
        middle_list.append(middle_part)
        normed_two_list.append(normed_two_part)
        pre_list.append(pre_part)
        act_list.append(act_part)
        next_list.append(next_part)
    middle = jnp.concatenate(middle_list, axis=0)
    normed_two = jnp.concatenate(normed_two_list, axis=0)
    pre_act = jnp.concatenate(pre_list, axis=0)
    activated = jnp.concatenate(act_list, axis=0)
    saved = [
        (
            hidden,
            normed,
            queries,
            keys_all,
            values_all,
            log_totals,
            attended,
            middle,
            normed_two,
            pre_act,
            activated,
        )
    ]
    hidden = jnp.concatenate(next_list, axis=0)
    final_out = hidden.astype(jnp.bfloat16)[None]
    grad_hidden = out_grad[0].astype(jnp.float32)
    shard_grads = [None] * LAYERS
    for layer_index in reversed(range(LAYERS)):
        (
            hidden_in,
            normed,
            queries,
            keys_all,
            values_all,
            log_totals,
            attended,
            middle,
            normed_two,
            pre_act,
            activated,
        ) = saved[layer_index]
        rest_sums = None
        middle_grads, attended_grads = ([], [])
        for part in range(2):
            out_matrix = lax.all_gather(out_weight[layer_index], ("dp", "seq"), axis=0, tiled=True)
            second_gain = lax.all_gather(ln2_gain[layer_index], ("dp", "seq"), axis=0, tiled=True)
            fc_matrix = lax.all_gather(fc_weight[layer_index], ("dp", "seq"), axis=0, tiled=True)
            proj_matrix = lax.all_gather(
                proj_weight[layer_index], ("dp", "seq"), axis=0, tiled=True
            )
            grad_next = rows_of(grad_hidden, part)
            grad_branch = grad_next.astype(jnp.bfloat16)
            grad_proj_shift = column_sum(grad_branch)
            grad_proj_matrix = left_product(rows_of(activated, part), grad_branch)
            grad_act = right_product(grad_branch, proj_matrix)
            gelu_back = jax.vjp(gelu_tanh, rows_of(pre_act, part))[1]
            grad_pre = gelu_back(grad_act)[0].astype(jnp.bfloat16)
            grad_fc_shift = column_sum(grad_pre)
            grad_fc_matrix = left_product(rows_of(normed_two, part), grad_pre)
            grad_normed_two = right_product(grad_pre, fc_matrix)
            gain_two = second_gain.astype(jnp.float32)
            second_back = jax.vjp(
                layer_norm, rows_of(middle, part), gain_two, jnp.zeros_like(gain_two)
            )[1]
            grad_middle_part, grad_second_gain, grad_second_shift = second_back(grad_normed_two)
            grad_middle = grad_next + grad_middle_part
            grad_attn = grad_middle.astype(jnp.bfloat16)
            grad_out_shift = column_sum(grad_attn)
            grad_out_matrix = left_product(rows_of(attended, part), grad_attn)
            attended_grads.append(right_product(grad_attn, out_matrix).astype(jnp.bfloat16))
            middle_grads.append(grad_middle)
            part_grads = (
                grad_out_matrix,
                grad_out_shift,
                grad_second_gain,
                grad_second_shift,
                grad_fc_matrix,
                grad_fc_shift,
                grad_proj_matrix,
                grad_proj_shift,
            )
            rest_sums = (
                part_grads
                if part == 0
                else tuple((total + term for total, term in zip(rest_sums, part_grads)))
            )
        grad_attended = jnp.concatenate(attended_grads, axis=0)
        query_terms, key_terms, value_terms = attend_backward(
            queries, keys_all, values_all, allowed, log_totals, grad_attended
        )
        key_part, value_part = (
            lax.psum_scatter(
                key_terms.astype(jnp.bfloat16), "seq", scatter_dimension=1, tiled=True
            ).astype(jnp.float32),
            lax.psum_scatter(
                value_terms.astype(jnp.bfloat16), "seq", scatter_dimension=1, tiled=True
            ).astype(jnp.float32),
        )
        grad_queries = side_by_side(query_terms, row_count).astype(jnp.bfloat16)
        grad_keys = side_by_side(key_part, row_count).astype(jnp.bfloat16)
        grad_values = side_by_side(value_part, row_count).astype(jnp.bfloat16)
        grad_query_shift = column_sum(grad_queries)
        grad_value_shift = column_sum(grad_values)
        grad_qkv = jnp.concatenate([grad_queries, grad_keys, grad_values], axis=1)
        input_sums = None
        hidden_grads = []
        for part in range(2):
            first_gain = lax.all_gather(ln1_gain[layer_index], ("dp", "seq"), axis=0, tiled=True)
            qkv_matrix = lax.all_gather(qkv_weight[layer_index], ("dp", "seq"), axis=0, tiled=True)
            grad_qkv_part = rows_of(grad_qkv, part)
            grad_qkv_matrix = left_product(rows_of(normed, part), grad_qkv_part)
            grad_normed = right_product(grad_qkv_part, qkv_matrix)
            gain_one = first_gain.astype(jnp.float32)
            first_back = jax.vjp(
                layer_norm, rows_of(hidden_in, part), gain_one, jnp.zeros_like(gain_one)
            )[1]
            grad_hidden_part, grad_first_gain, grad_first_shift = first_back(grad_normed)
            hidden_grads.append(middle_grads[part] + grad_hidden_part)
            part_grads = (grad_first_gain, grad_first_shift, grad_qkv_matrix)
            input_sums = (
                part_grads
                if part == 0
                else tuple((total + term for total, term in zip(input_sums, part_grads)))
            )
        grad_hidden = jnp.concatenate(hidden_grads, axis=0)
        shard_grads[layer_index] = (
            lax.psum_scatter(input_sums[0], ("dp", "seq"), scatter_dimension=0, tiled=True),
            lax.psum_scatter(input_sums[1], ("dp", "seq"), scatter_dimension=0, tiled=True),
            lax.psum_scatter(input_sums[2], ("dp", "seq"), scatter_dimension=0, tiled=True),
            lax.psum_scatter(grad_query_shift, ("dp", "seq"), scatter_dimension=0, tiled=True),
            lax.psum_scatter(grad_value_shift, ("dp", "seq"), scatter_dimension=0, tiled=True),
            lax.psum_scatter(rest_sums[0], ("dp", "seq"), scatter_dimension=0, tiled=True),
            lax.psum_scatter(rest_sums[1], ("dp", "seq"), scatter_dimension=0, tiled=True),
            lax.psum_scatter(rest_sums[2], ("dp", "seq"), scatter_dimension=0, tiled=True),
            lax.psum_scatter(rest_sums[3], ("dp", "seq"), scatter_dimension=0, tiled=True),
            lax.psum_scatter(rest_sums[4], ("dp", "seq"), scatter_dimension=0, tiled=True),
            lax.psum_scatter(rest_sums[5], ("dp", "seq"), scatter_dimension=0, tiled=True),
            lax.psum_scatter(rest_sums[6], ("dp", "seq"), scatter_dimension=0, tiled=True),
            lax.psum_scatter(rest_sums[7], ("dp", "seq"), scatter_dimension=0, tiled=True),
        )
    stacked = []
    for member in range(13):
        stacked.append(jnp.stack([layer_grads[member] for layer_grads in shard_grads], axis=0))
    return (final_out, grad_hidden[None]) + tuple(stacked)


def solution(mesh):
    placed = (
        P("dp", "seq", None),
        P("dp", "seq", None),
        P("dp", None),
        P("dp", None),
        P(None, ("dp", "seq")),
        P(None, ("dp", "seq")),
        P(None, ("dp", "seq"), None),
        P(None, ("dp", "seq")),
        P(None, ("dp", "seq")),
        P(None, ("dp", "seq"), None),
        P(None, ("dp", "seq")),
        P(None, ("dp", "seq")),
        P(None, ("dp", "seq")),
        P(None, ("dp", "seq"), None),
        P(None, ("dp", "seq")),
        P(None, ("dp", "seq"), None),
        P(None, ("dp", "seq")),
    )
    return jax.shard_map(
        on_device,
        mesh=mesh,
        in_specs=placed,
        out_specs=(
            P("dp", "seq", None),
            P("dp", "seq", None),
            P(None, ("dp", "seq")),
            P(None, ("dp", "seq")),
            P(None, ("dp", "seq"), None),
            P(None, ("dp", "seq")),
            P(None, ("dp", "seq")),
            P(None, ("dp", "seq"), None),
            P(None, ("dp", "seq")),
            P(None, ("dp", "seq")),
            P(None, ("dp", "seq")),
            P(None, ("dp", "seq"), None),
            P(None, ("dp", "seq")),
            P(None, ("dp", "seq"), None),
            P(None, ("dp", "seq")),
        ),
        check_vma=False,
    )
```

profile of v0, /device:TPU:0, one launch (start us, length us, event | category | flops | bytes accessed | tf_op | source)
XLA Modules:
  0.0 4771.6 jit_solution(3044427373469220231)
XLA Ops:
  15.5 68.7 %all-reduce.19 = (bf16[1024]{0:T(1024)(128)(2,1)S(1)}, bf16[1024]{0:T(1024)(128)(2,1)S(1)}, bf16[1024]{0:T(1024)(128)(2,1)S(1)}, bf16[1024]{0:T(1024)(128)(2,1)S...) all-reduce(bf16[1024]{0:T(1024)(128)(2,1)S(1)} %dynamic-update-slic, ...), channel_id=3, replica_groups=mesh['dp'=4,'seq'=32] {'dp','seq'}, use_global_device_ids=true, to_apply=%add.1 | all-reduce | flops 12288 | bytes 49152
  85.7 235.9 %all-gather.24.cloned.1.call-done = bf16[1,1024,3072]{2,1,0:T(8,128)(2,1)} async-done(((bf16[1,8,3072]{2,1,0:T(8,128)(2,1)}), bf16[1,1024,3072]{2,1,0:T(8,128)(2,1)}) %all-gather.24.cloned.1.call-update) | async-done | bytes 6291472 | tf_op jit(solution)/shard_map/all_gather | solution.py:184
  331.9 165.5 %all-gather.22.cloned.1.call-done = bf16[4096,1024]{1,0:T(8,128)(2,1)} async-done(((bf16[128,1024]{1,0:T(8,128)(2,1)}), bf16[4096,1024]{1,0:T(8,128)(2,1)}) %all-gather.22.cloned.1.call-update) | async-done | bytes 8388624 | tf_op jit(solution)/shard_map/all_gather | solution.py:201
  497.3 11.3 copy.48
  508.6 159.2 %all-gather.20.cloned.1.call-done = bf16[4096,1024]{1,0:T(8,128)(2,1)} async-done(((bf16[128,1024]{1,0:T(8,128)(2,1)}), bf16[4096,1024]{1,0:T(8,128)(2,1)}) %all-gather.20.cloned.1.call-update) | async-done | bytes 8388624 | tf_op jit(solution)/shard_map/all_gather | solution.py:202
  667.8 11.5 copy.46
  679.3 62.4 %while.28 = (s32[]{:T(128)}, bf16[8,128,128]{1,2,0:T(8,128)(2,1)S(1)}, f32[8,2,128]{2,1,0:T(2,128)S(1)}, bf16[4096,1024]{0,1:T(8,128)(2,1)}, s32[8]{0:T(128)S(1)...) while((s32[]{:T(128)}, ...), condition=%wide.region_9.10_spmd.clone, body=%wide.region_6.9_spmd.clone.sunk | while | flops 278920960 | bytes 20161876 | solution.py:91
  742.6 227.2 %all-gather.26.cloned.1.call-done = bf16[1,1024,1024]{2,1,0:T(8,128)(2,1)} async-done(((bf16[1,8,1024]{2,1,0:T(8,128)(2,1)}), bf16[1,1024,1024]{2,1,0:T(8,128)(2,1)}) %all-gather.26.cloned.1.call-update) | async-done | bytes 2097168 | tf_op jit(solution)/shard_map/all_gather | solution.py:211
  974.7 309.4 %all-gather.28.cloned.1.call-done = bf16[1,1024,4096]{2,1,0:T(8,128)(2,1)} async-done(((bf16[1,8,4096]{2,1,0:T(8,128)(2,1)}), bf16[1,1024,4096]{2,1,0:T(8,128)(2,1)}) %all-gather.28.cloned.1.call-update) | async-done | bytes 8388624 | tf_op jit(solution)/shard_map/all_gather | solution.py:215
  1291.5 306.6 %all-gather.30.cloned.1.call-done = bf16[1,4096,1024]{2,1,0:T(8,128)(2,1)} async-done(((bf16[1,32,1024]{2,1,0:T(8,128)(2,1)}), bf16[1,4096,1024]{2,1,0:T(8,128)(2,1)}) %all-gather.30.cloned.1.call-update) | async-done | bytes 8388624 | tf_op jit(solution)/shard_map/all_gather | solution.py:217
  1621.7 117.5 %while.29 = (s32[]{:T(128)}, bf16[8,128,128]{1,2,0:T(8,128)(2,1)}, bf16[8,4096,128]{1,2,0:T(8,128)(2,1)}, bf16[8,4096,128]{1,2,0:T(8,128)(2,1)}, bf16[4096,1024]...) while((s32[]{:T(128)}, bf16[8,128,128]{1,2,0:T(8,128)(2,1)}, ...), condition=%wide.region_20.21_spmd.clone, body=%wide.region_18.20_spmd.clone.sunk | while | flops 683704064 | bytes 46537080 | solution.py:131
  1739.2 12.1 copy.55
  1751.3 8.7 copy.63
  1760.1 12.1 copy.53
  1772.2 8.8 copy.64
  1788.1 8.1 convolution_add_fusion
  1799.7 8.2 convolution_add_fusion.1
  1808.2 133.0 %reduce-scatter.21.cloned.1.call-done = bf16[128,1024]{1,0:T(8,128)(2,1)} async-done(((bf16[4096,1024]{1,0:T(8,128)(2,1)}), bf16[128,1024]{1,0:T(8,128)(2,1)}) %reduce-scatter.21.cloned.1.call-update) | async-done | bytes 262160
  1943.1 176.0 %reduce-scatter.19.cloned.1.call-done = bf16[128,1024]{1,0:T(8,128)(2,1)} async-done(((bf16[4096,1024]{1,0:T(8,128)(2,1)}), bf16[128,1024]{1,0:T(8,128)(2,1)}) %reduce-scatter.19.cloned.1.call-update) | async-done | bytes 262160
  2148.4 64.7 %all-reduce.18 = (f32[1024]{0:T(1024)S(1)}, f32[1024]{0:T(1024)S(1)}, f32[1024]{0:T(1024)S(1)}, f32[1024]{0:T(1024)S(1)}, f32[1024]{0:T(1024)S(1)}, /*index=5*/f...) all-reduce(f32[1024]{0:T(1024)S(1)} %add.370, ...), channel_id=17, replica_groups=mesh['dp'=4,'seq'=32] {'dp','seq'}, use_global_device_ids=true, to_apply=%region_29.30.clone | all-reduce | flops 12288 | bytes 98304
  2219.2 543.1 %reduce-scatter.13.cloned.1.call-done = f32[8,1024]{1,0:T(8,128)} async-done(((f32[1024,1024]{1,0:T(8,128)}), f32[8,1024]{1,0:T(8,128)}) %reduce-scatter.13.cloned.1.call-update) | async-done | bytes 32784 | tf_op jit(solution)/shard_map/reduce_scatter | solution.py:364
  2762.3 671.1 %reduce-scatter.17.cloned.1.call-done = f32[32,1024]{1,0:T(8,128)} async-done(((f32[4096,1024]{1,0:T(8,128)}), f32[32,1024]{1,0:T(8,128)}) %reduce-scatter.17.cloned.1.call-update) | async-done | bytes 131088 | tf_op jit(solution)/shard_map/reduce_scatter | solution.py:370
  3433.4 671.1 %reduce-scatter.15.cloned.1.call-done = f32[8,4096]{1,0:T(8,128)} async-done(((f32[1024,4096]{1,0:T(8,128)}), f32[8,4096]{1,0:T(8,128)}) %reduce-scatter.15.cloned.1.call-update) | async-done | bytes 131088 | tf_op jit(solution)/shard_map/reduce_scatter | solution.py:368
  4104.5 659.9 %reduce-scatter.11.cloned.1.call-done = f32[8,3072]{1,0:T(8,128)} async-done(((f32[1024,3072]{1,0:T(8,128)}), f32[8,3072]{1,0:T(8,128)}) %reduce-scatter.11.cloned.1.call-update) | async-done | bytes 98320 | tf_op jit(solution)/shard_map/reduce_scatter | solution.py:361
  (465 shorter events, 251.6 us)
Async XLA Ops:
  7.2 314.4 %all-gather.24.cloned.1.call-start = ((), (), s32[]{:S(2)}) async-start(), calls=%async_computation.12 | async-start | bytes 6340608 | tf_op jit(solution)/shard_map/all_gather | solution.py:184
  7.9 489.4 %all-gather.22.cloned.1.call-start = ((), (), s32[]{:S(2)}) async-start(), calls=%async_computation.7 | async-start | bytes 8650752 | tf_op jit(solution)/shard_map/all_gather | solution.py:201
  85.2 887.0 %copy-start.4 = (f32[1,128,1024]{2,1,0:T(8,128)}, f32[1,128,1024]{2,1,0:T(8,128)S(1)}, u32[]{:S(2)}) copy-start(f32[1,128,1024]{2,1,0:T(8,128)S(1)} %convert_element_type.191) | copy-start | bytes 1572868
  85.4 242.1 %copy-start.30 = (f32[64]{0:T(128)}, f32[64]{0:T(128)S(1)}, u32[]{:S(2)}) copy-start(f32[64]{0:T(128)S(1)} %get-tuple-element.413) | copy-start | bytes 772
  85.6 241.9 %copy-start.52 = (f32[64]{0:T(128)}, f32[64]{0:T(128)S(1)}, u32[]{:S(2)}) copy-start(f32[64]{0:T(128)S(1)} %get-tuple-element.283) | copy-start | bytes 772
  85.6 241.9 %copy-start.54 = (f32[64]{0:T(128)}, f32[64]{0:T(128)S(1)}, u32[]{:S(2)}) copy-start(f32[64]{0:T(128)S(1)} %get-tuple-element.284) | copy-start | bytes 772
  328.3 339.5 %all-gather.20.cloned.1.call-start = ((), (), s32[]{:S(2)}) async-start(), calls=%async_computation.6 | async-start | bytes 8650752 | tf_op jit(solution)/shard_map/all_gather | solution.py:202
  329.2 640.6 %all-gather.26.cloned.1.call-start = ((), (), s32[]{:S(2)}) async-start(), calls=%async_computation.13 | async-start | bytes 2113536 | tf_op jit(solution)/shard_map/all_gather | solution.py:211
  329.8 954.3 %all-gather.28.cloned.1.call-start = ((), (), s32[]{:S(2)}) async-start(), calls=%async_computation.14 | async-start | bytes 8454144 | tf_op jit(solution)/shard_map/all_gather | solution.py:215
  330.4 1267.7 %all-gather.30.cloned.1.call-start = ((), (), s32[]{:S(2)}) async-start(), calls=%async_computation.15 | async-start | bytes 8454144 | tf_op jit(solution)/shard_map/all_gather | solution.py:217
  331.0 1610.2 %reduce-scatter.21.cloned.1.call-start = ((), (), s32[]{:S(2)}) async-start(), calls=%async_computation.17 | async-start | bytes 8650752
  742.6 541.5 %copy-start.8 = (bf16[64,8,128]{0,2,1:T(8,128)(2,1)}, bf16[64,8,128]{0,2,1:T(8,128)(2,1)S(1)}, u32[]{:S(2)}) copy-start(bf16[64,8,128]{0,2,1:T(8,128)(2,1)S(1)} %get-tuple-element.394) | copy-start | bytes 393220
  742.6 541.5 %copy-start.10 = (bf16[64,8,128]{0,2,1:T(8,128)(2,1)}, bf16[64,8,128]{0,2,1:T(8,128)(2,1)S(1)}, u32[]{:S(2)}) copy-start(bf16[64,8,128]{0,2,1:T(8,128)(2,1)S(1)} %get-tuple-element.393) | copy-start | bytes 393220
  1291.5 496.6 %copy-start.6 = (f32[64,4096]{1,0:T(8,128)}, f32[64,4096]{1,0:T(8,128)S(1)}, u32[]{:S(2)}) copy-start(f32[64,4096]{1,0:T(8,128)S(1)} %fusion.40) | copy-start | bytes 3145732
  1760.0 359.0 %reduce-scatter.19.cloned.1.call-start = ((), (), s32[]{:S(2)}) async-start(), calls=%async_computation.16 | async-start | bytes 8650752
  1781.0 981.3 %reduce-scatter.13.cloned.1.call-start = ((), (), s32[]{:S(2)}) async-start(), calls=%async_computation.9 | async-start | bytes 4227072 | tf_op jit(solution)/shard_map/reduce_scatter | solution.py:364
  1785.6 1647.8 %reduce-scatter.17.cloned.1.call-start = ((), (), s32[]{:S(2)}) async-start(), calls=%async_computation.11 | async-start | bytes 16908288 | tf_op jit(solution)/shard_map/reduce_scatter | solution.py:370
  1796.2 2308.2 %reduce-scatter.15.cloned.1.call-start = ((), (), s32[]{:S(2)}) async-start(), calls=%async_computation.10 | async-start | bytes 16908288 | tf_op jit(solution)/shard_map/reduce_scatter | solution.py:368
  1807.9 314.3 %copy-start.5 = (f32[1,128,1024]{2,1,0:T(8,128)S(1)}, f32[1,128,1024]{2,1,0:T(8,128)}, u32[]{:S(2)}) copy-start(f32[1,128,1024]{2,1,0:T(8,128)} %copy-done.4) | copy-start | bytes 1572868
  1807.9 314.3 %copy-start.26 = (f32[1024]{0:T(1024)S(1)}, f32[1024]{0:T(1024)}, u32[]{:S(2)}) copy-start(f32[1024]{0:T(1024)} %copy-done.25) | copy-start | bytes 12292
  1807.9 314.3 %copy-start.29 = (f32[1024]{0:T(1024)S(1)}, f32[1024]{0:T(1024)}, u32[]{:S(2)}) copy-start(f32[1024]{0:T(1024)} %copy-done.28) | copy-start | bytes 12292
  1807.9 314.3 %copy-start.31 = (f32[64]{0:T(128)S(1)}, f32[64]{0:T(128)}, u32[]{:S(2)}) copy-start(f32[64]{0:T(128)} %copy-done.30) | copy-start | bytes 772
  1807.9 314.3 %copy-start.43 = (f32[64]{0:T(128)S(1)}, f32[64]{0:T(128)}, u32[]{:S(2)}) copy-start(f32[64]{0:T(128)} %copy-done.42) | copy-start | bytes 772
  1807.9 2956.5 %reduce-scatter.11.cloned.1.call-start = ((), (), s32[]{:S(2)}) async-start(), calls=%async_computation.8 | async-start | bytes 12681216 | tf_op jit(solution)/shard_map/reduce_scatter | solution.py:361
  (49 other events, 1355.7 us)
Sparse Core Ops, SparseCore 0:
  9.7 311.8 all-gather.23
  328.4 168.8 all-gather.21
  499.5 168.1 all-gather.19
  669.3 300.4 all-gather.25
  971.4 312.6 all-gather.27
  1285.6 312.4 all-gather.29
  1760.2 180.9 reduce-scatter.20
  1943.6 175.4 reduce-scatter.18
  2122.0 640.2 reduce-scatter.12
  2765.2 668.1 reduce-scatter.16
  3436.5 667.9 reduce-scatter.14
  4107.4 656.9 reduce-scatter.10
where the time goes:
time: 4780 us; the launch traced here: 4770 us
  waiting for transfers between devices  4260 us (89%)
  local copies, waits for them, and re-layouts  160 us (3%)
  matrix products  137 us (3%)
  blocking collectives  133 us (3%)
    reduce_scatter x1, waiting for transfers between devices, on_device(): lax.psum_scatter(rest_sums[6], ('dp', 'seq'), scatter_dimension=0, tiled=...  671 us
    reduce_scatter x1, waiting for transfers between devices, on_device(): lax.psum_scatter(rest_sums[4], ('dp', 'seq'), scatter_dimension=0, tiled=...  671 us
    reduce_scatter x1, waiting for transfers between devices, on_device(): lax.psum_scatter(input_sums[2], ('dp', 'seq'), scatter_dimension=0, tiled...  660 us
    reduce_scatter x1, waiting for transfers between devices, on_device(): lax.psum_scatter(rest_sums[0], ('dp', 'seq'), scatter_dimension=0, tiled=...  543 us
    unnamed x14, waiting for transfers between devices  311 us
    all_gather x1, waiting for transfers between devices, on_device(): lax.all_gather(fc_weight[layer_index], ('dp', 'seq'), axis=0, tiled=True)  309 us
    all_gather x1, waiting for transfers between devices, on_device(): lax.all_gather(proj_weight[layer_index], ('dp', 'seq'), axis=0, tiled=True)  307 us
    all_gather x1, waiting for transfers between devices, on_device(): lax.all_gather(qkv_weight[layer_index], ('dp', 'seq'), axis=0, tiled=True)  236 us
  transfers between devices with their start and end apart: 12, of which 12 were waited for; matrix products, arithmetic and copies ran while one was open for 4% of the time, Pallas kernels for 0%

commit v1 on v0

v1 whole, which is shorter than its diff:
```python
import functools

import jax
import jax.numpy as jnp
from jax import lax
from jax.experimental import pallas as pl
from jax.experimental.pallas import tpu as pltpu
from jax.sharding import Mesh, PartitionSpec as P

D = 1024
PIECE = 256
EPS = 1e-05
NEG = -1e30
LOG2E = 1.4426950408889634
BF = jnp.bfloat16
F32 = jnp.float32
AXES = ("yh", "core", "yl", "x", "z")
Y = ("yh", "yl")
QB = 256
KB = 512


def plain_product(left_side, right_side):
    return jnp.dot(left_side, right_side, preferred_element_type=F32)


def left_product(left_side, right_side):
    return lax.dot_general(
        left_side, right_side, (((0,), (0,)), ((), ())), preferred_element_type=F32
    )


def right_product(left_side, right_side):
    return lax.dot_general(
        left_side, right_side, (((1,), (1,)), ((), ())), preferred_element_type=F32
    )


def gelu_tanh(values):
    return (
        0.5
        * values
        * (1.0 + jnp.tanh(0.7978845608028654 * (values + 0.044715 * values * values * values)))
    )


def layer_norm(values, gain, shift):
    center = values - jnp.mean(values, axis=-1, keepdims=True)
    spread = jnp.mean(center * center, axis=-1, keepdims=True)
    return center * lax.rsqrt(spread + EPS) * gain + shift


def norm_backward(values, gain, grad):
    center = values - jnp.mean(values, axis=-1, keepdims=True)
    spread = jnp.mean(center * center, axis=-1, keepdims=True)
    scale = lax.rsqrt(spread + EPS)
    normed = center * scale
    pulled = grad * gain
    back = scale * (
        pulled
        - jnp.mean(pulled, axis=-1, keepdims=True)
        - normed * jnp.mean(pulled * normed, axis=-1, keepdims=True)
    )
    return back, normed


def shift(values, axis, step):
    return lax.ppermute(values, axis, [(i, (i + step) % 4) for i in range(4)])


def swap_core(values):
    return lax.ppermute(values, "core", [(0, 1), (1, 0)])


def ring_blocks(values, axis):
    return [values, shift(values, axis, -1), shift(values, axis, 2), shift(values, axis, 1)]


def ring_stack(values, axis):
    return jnp.stack(ring_blocks(values, axis))


def place_call(kernel, places, blocks, shapes):
    return pl.pallas_call(
        kernel,
        out_shape=[jax.ShapeDtypeStruct(shape, BF) for shape in shapes],
        in_specs=[pl.BlockSpec(memory_space=pltpu.SMEM)]
        + [pl.BlockSpec(memory_space=pltpu.VMEM)] * len(blocks),
        out_specs=[pl.BlockSpec(memory_space=pltpu.VMEM)] * len(shapes),
        compiler_params=pltpu.CompilerParams(vmem_limit_bytes=48 * 1024 * 1024),
    )(places, *blocks)


def around(place, step):
    return lax.rem(place + step, 4)


def feature_row(y, side, x):
    return pl.multiple_of((y // 2) * 512 + side * 256 + (y % 2) * 128 + x * 32, 32)


def place_first(places, *refs):
    sources, out = refs[:4], refs[4]
    for step in range(4):
        y = around(places[0], step)

        @pl.loop(0, 4)
        def _(turn):
            x = around(places[1], turn)
            for side in range(2):
                out[pl.ds(feature_row(y, side, x), 32), :] = sources[step][
                    turn, side * 32 : side * 32 + 32, :
                ]


def place_second(places, *refs):
    sources, fc, out = refs[:4], refs[4], refs[5]
    for step in range(4):
        z = around(places[2], step)
        columns = pl.ds(pl.multiple_of(z * 256, 256), 256)

        @pl.loop(0, 16)
        def _(turn):
            y, x = around(places[0], turn // 4), around(places[1], turn % 4)
            for side in range(2):
                fc[z, pl.ds(feature_row(y, side, x), 32), :] = sources[step][
                    turn // 4, turn % 4, side * 32 : side * 32 + 32, :
                ]
            row = pl.multiple_of((y * 4 + x) * 32, 32)
            block = sources[step][turn // 4, turn % 4, 64:80, :]
            out[pl.ds(row, 16), columns] = block[:, :256]
            out[pl.ds(row + 16, 16), columns] = block[:, 256:]


def place_third(places, *refs):
    sources, out = refs[:4], refs[4]
    for step in range(4):
        y = around(places[0], step)

        @pl.loop(0, 16)
        def _(turn):
            x, z = around(places[1], turn // 4), around(places[2], turn % 4)
            out[y, pl.ds(pl.multiple_of((x * 4 + z) * 32, 32), 32), :] = sources[step][
                turn // 4, turn % 4
            ]


def place_rows(places, own, other, out):
    for step in range(4):
        z = around(places[2], step)
        out[places[3], z] = own[step]
        out[1 - places[3], z] = other[step]


def ring_reduce(values, axis):
    place = lax.axis_index(axis)

    def block(step):
        return lax.dynamic_index_in_dim(values, (place + step) % 4, 0, keepdims=False)

    total = (
        block(0).astype(F32)
        + shift(block(1), axis, 1).astype(F32)
        + shift(block(2), axis, 2).astype(F32)
        + shift(block(3), axis, -1).astype(F32)
    )
    return total.astype(values.dtype)


def limit_of(position, starts):
    limit = position
    for start in starts:
        limit = jnp.where((position >= start) & (position < start + PIECE), start + PIECE - 1, limit)
    return limit


def lane_half(shape):
    return lax.broadcasted_iota(jnp.int32, shape, 1) < 64


def forward_kernel(
    order_ref, source_ref, where_ref, starts_ref, got_ref, kv_ref, q_ref, o_ref, lse_ref, msg_ref
):
    starts = [starts_ref[i] for i in range(6)]

    @pl.loop(0, 64)
    def _(span):
        stored = order_ref[span]
        kv_ref[pl.ds(pl.multiple_of(span * 64, 64), 64), :] = got_ref[
            stored // 8, pl.ds(pl.multiple_of((stored % 8) * 64, 64), 64), :
        ]

    @pl.loop(0, 32)
    def _(span):
        source = source_ref[span]
        packed = got_ref[
            source // 4, pl.ds(pl.multiple_of(512 + (source % 4) * 32, 32), 32), :
        ].astype(F32) * 0.125
        left = lane_half(packed.shape)
        row = pl.multiple_of(span * 64, 64)
        q_ref[pl.ds(row, 32), :] = jnp.where(left, packed, 0.0).astype(BF)
        q_ref[pl.ds(row + 32, 32), :] = jnp.where(left, pltpu.roll(packed, 64, 1), 0.0).astype(BF)

    @pl.loop(0, 2048 // QB)
    def _(block):
        row = pl.multiple_of(block * QB, QB)
        query = q_ref[pl.ds(row, QB), :]
        spans = QB // 64
        first = limit_of(where_ref[block * spans] * 64, starts)
        last = limit_of(where_ref[block * spans + spans - 1] * 64 + 63, starts)
        full = (first + 1) // KB
        count = last // KB + 1
        inner = lax.broadcasted_iota(jnp.int32, (64, 1), 0)
        position = jnp.concatenate(
            [where_ref[block * spans + i] * 64 + inner for i in range(spans)], axis=0
        )
        limit = limit_of(position, starts)

        def step(masked, index, carry):
            maxima, totals, mixture = carry
            begin = pl.multiple_of(index * KB, KB)
            pair = kv_ref[pl.ds(begin, KB), :]
            scores = right_product(query, pair)
            if masked:
                key_pos = begin + lax.broadcasted_iota(jnp.int32, (1, KB), 1)
                scores = jnp.where(key_pos <= limit, scores, NEG)
            higher = jnp.maximum(maxima, jnp.max(scores, axis=1, keepdims=True))
            raised = jnp.exp2((scores - higher) * LOG2E)
            fade = jnp.exp2((maxima - higher) * LOG2E)
            totals = totals * fade + jnp.sum(raised, axis=1, keepdims=True)
            mixture = mixture * fade + plain_product(raised.astype(BF), pair)
            return higher, totals, mixture

        carry = (
            jnp.full((QB, 1), NEG, F32),
            jnp.zeros((QB, 1), F32),
            jnp.zeros((QB, 128), F32),
        )
        carry = lax.fori_loop(0, full, functools.partial(step, False), carry)
        maxima, totals, mixture = lax.fori_loop(full, count, functools.partial(step, True), carry)
        attended = mixture / totals
        o_ref[pl.ds(row, QB), :] = attended.astype(BF)
        log_total = maxima * LOG2E + jnp.log2(totals)
        lse_ref[block] = jnp.transpose(jnp.broadcast_to(log_total, (QB, 128)))[0:8, :]
        turned = pltpu.roll(attended, 64, 1)
        for i in range(spans):
            top, bottom = turned[i * 64 : i * 64 + 32], attended[i * 64 + 32 : i * 64 + 64]
            msg_ref[source_ref[block * spans + i]] = jnp.where(
                lane_half(top.shape), top, bottom
            ).astype(BF)


def backward_kernel(
    order_ref,
    source_ref,
    where_ref,
    starts_ref,
    kv_ref,
    q_ref,
    o_ref,
    lse_ref,
    got_ref,
    msg_ref,
    do_ref,
    sum_ref,
):
    starts = [starts_ref[i] for i in range(6)]

    @pl.loop(0, 32)
    def _(span):
        packed = got_ref[source_ref[span]].astype(F32)
        left = lane_half(packed.shape)
        row = pl.multiple_of(span * 64, 64)
        do_ref[pl.ds(row, 32), :] = jnp.where(left, 0.0, pltpu.roll(packed, 64, 1)).astype(BF)
        do_ref[pl.ds(row + 32, 32), :] = jnp.where(left, 0.0, packed).astype(BF)

    sum_ref[...] = jnp.zeros_like(sum_ref)

    @pl.loop(0, 2048 // QB)
    def _(block):
        row = pl.multiple_of(block * QB, QB)
        query = q_ref[pl.ds(row, QB), :]
        grad = do_ref[pl.ds(row, QB), :]
        both = jnp.concatenate([query, grad], axis=0)
        spans = QB // 64
        first = limit_of(where_ref[block * spans] * 64, starts)
        last = limit_of(where_ref[block * spans + spans - 1] * 64 + 63, starts)
        full = (first + 1) // KB
        count = last // KB + 1
        inner = lax.broadcasted_iota(jnp.int32, (1, 64), 1)
        position = jnp.concatenate(
            [where_ref[block * spans + i] * 64 + inner for i in range(spans)], axis=1
        )
        limit = limit_of(position, starts)
        log_total = lse_ref[block][0:1, :]
        product = grad.astype(F32) * o_ref[pl.ds(row, QB), :].astype(F32)
        delta = lax.dot_general(
            jnp.ones((8, 128), F32),
            product,
            (((1,), (1,)), ((), ())),
            precision=lax.Precision.HIGHEST,
            preferred_element_type=F32,
        )[0:1, :]

        def step(masked, index, total):
            begin = pl.multiple_of(index * KB, KB)
            pair = kv_ref[pl.ds(begin, KB), :]
            scores = right_product(pair, query)
            if masked:
                key_pos = begin + lax.broadcasted_iota(jnp.int32, (KB, 1), 0)
                scores = jnp.where(key_pos <= limit, scores, NEG)
            weights = jnp.exp2(scores * LOG2E - log_total)
            grad_scores = (weights * (right_product(pair, grad) - delta)).astype(BF)
            sum_ref[pl.ds(begin, KB), :] += plain_product(
                jnp.concatenate([grad_scores, weights.astype(BF)], axis=1), both
            )
            return total + left_product(grad_scores, pair)

        total = jnp.zeros((QB, 128), F32)
        total = lax.fori_loop(0, full, functools.partial(step, False), total)
        total = lax.fori_loop(full, count, functools.partial(step, True), total) * 0.125
        turned = pltpu.roll(total, 64, 1)
        for i in range(spans):
            top, bottom = total[i * 64 : i * 64 + 32], turned[i * 64 + 32 : i * 64 + 64]
            source = source_ref[block * spans + i]
            msg_ref[
                source // 4, pl.ds(pl.multiple_of(512 + (source % 4) * 32, 32), 32), :
            ] = jnp.where(lane_half(top.shape), top, bottom).astype(BF)

    @pl.loop(0, 64)
    def _(span):
        stored = order_ref[span]
        msg_ref[stored // 8, pl.ds(pl.multiple_of((stored % 8) * 64, 64), 64), :] = sum_ref[
            pl.ds(pl.multiple_of(span * 64, 64), 64), :
        ].astype(BF)


def attend_forward(tables, got):
    shapes = [
        jax.ShapeDtypeStruct((4096, 128), BF),
        jax.ShapeDtypeStruct((2048, 128), BF),
        jax.ShapeDtypeStruct((2048, 128), BF),
        jax.ShapeDtypeStruct((2048 // QB, 8, QB), F32),
        jax.ShapeDtypeStruct((32, 32, 128), BF),
    ]
    return pl.pallas_call(
        forward_kernel,
        out_shape=shapes,
        in_specs=[pl.BlockSpec(memory_space=pltpu.SMEM)] * 4
        + [pl.BlockSpec(memory_space=pltpu.VMEM)],
        out_specs=[pl.BlockSpec(memory_space=pltpu.VMEM)] * 5,
        compiler_params=pltpu.CompilerParams(vmem_limit_bytes=48 * 1024 * 1024),
    )(*tables, got)


def attend_backward(tables, saved, got):
    return pl.pallas_call(
        backward_kernel,
        out_shape=jax.ShapeDtypeStruct((8, 640, 128), BF),
        in_specs=[pl.BlockSpec(memory_space=pltpu.SMEM)] * 4
        + [pl.BlockSpec(memory_space=pltpu.VMEM)] * 5,
        out_specs=pl.BlockSpec(memory_space=pltpu.VMEM),
        scratch_shapes=[pltpu.VMEM((2048, 128), BF), pltpu.VMEM((4096, 128), F32)],
        compiler_params=pltpu.CompilerParams(vmem_limit_bytes=48 * 1024 * 1024),
    )(*tables, *saved, got)


def order_tables(span_order, piece_starts, part):
    places = jnp.arange(64, dtype=jnp.int32)
    order = jnp.sum(jnp.where(span_order[None, :] == places[:, None], places[None, :], 0), axis=1)
    mine = lax.dynamic_index_in_dim(span_order.reshape(32, 2), part, 1, keepdims=False)
    rank = jnp.sum((mine[None, :] < mine[:, None]).astype(jnp.int32), axis=1)
    sources = jnp.arange(32, dtype=jnp.int32)
    hit = rank[None, :] == sources[:, None]
    source = jnp.sum(jnp.where(hit, sources[None, :], 0), axis=1)
    where = jnp.sum(jnp.where(hit, mine[None, :], 0), axis=1)
    return order.astype(jnp.int32), source.astype(jnp.int32), where.astype(jnp.int32), piece_starts


def on_device(
    tokens,
    out_grad,
    piece_starts,
    span_order,
    ln1_gain,
    ln1_bias,
    qkv_weight,
    query_bias,
    value_bias,
    out_weight,
    out_bias,
    ln2_gain,
    ln2_bias,
    fc_weight,
    fc_bias,
    proj_weight,
    proj_bias,
):
    core = lax.axis_index("core")
    z_place = lax.axis_index("z")
    x_place = lax.axis_index("x")
    y_place = lax.axis_index(Y)
    sequence = lax.axis_index("yl")
    head_part = x_place // 2
    query_part = x_place % 2
    places = jnp.stack([y_place, x_place, z_place, core]).astype(jnp.int32)
    own = tokens[0]
    dm_own = out_grad[0]

    both_tables = lax.all_gather(
        jnp.concatenate([span_order[0], piece_starts[0]]), "core", axis=0, tiled=False
    )
    table = lax.dynamic_index_in_dim(both_tables, sequence, 0, keepdims=False)
    tables = order_tables(table[:64], table[64:], query_part)

    qkv_parts = qkv_weight[0].reshape(8, 3, 2, 2, 2, 2, 64)
    kv_cols = qkv_parts[:, 1:].transpose(3, 2, 4, 0, 5, 1, 6).reshape(2, 4, 8, 256)
    q_cols = qkv_parts[:, 0].transpose(2, 1, 3, 0, 4, 5).reshape(2, 4, 8, 128)
    fc_cols = fc_weight[0].reshape(8, 2, 2, 2, 512).transpose(2, 1, 3, 0, 4).reshape(2, 4, 8, 512)
    out_cols = jnp.broadcast_to(
        out_weight[0].reshape(8, 4, 256).transpose(1, 0, 2)[None], (2, 4, 8, 256)
    )
    vectors = jnp.stack(
        [
            ln1_gain[0],
            ln1_bias[0],
            query_bias[0],
            value_bias[0],
            out_bias[0],
            ln2_gain[0],
            ln2_bias[0],
            proj_bias[0],
        ],
        axis=1,
    )
    vectors = jnp.concatenate(
        [vectors, fc_bias[0].reshape(8, 4), jnp.zeros((8, 116), BF)], axis=1
    )
    vec_cols = jnp.broadcast_to(vectors[None, None], (2, 4, 8, 128))
    packed = jnp.concatenate([kv_cols, q_cols, vec_cols, fc_cols, out_cols], axis=3)
    spread = lax.all_to_all(
        packed.reshape(8, 8, 1280), ("core", "z"), split_axis=0, concat_axis=0, tiled=True
    )

    first = ring_stack(spread[:, :, :512].reshape(64, 512), "x")
    first = place_call(place_first, places, ring_blocks(first, Y), [(1024, 512)])[0]
    qkv_matrix = first[:, :384]
    rows = first[:, 384:396].T
    first_gain, first_shift, q_shift, v_shift, out_shift, gain_two, shift_two, proj_shift = [
        rows[i].astype(F32) for i in range(8)
    ]
    fc_shift = first[:, 392:396].reshape(4096)

    out_mine = lax.dynamic_index_in_dim(
        spread[:, :, 1024:].reshape(2, 32, 256), core, 0, keepdims=False
    )
    out_mine = out_mine.reshape(2, 16, 256).transpose(1, 0, 2).reshape(16, 512)
    second = jnp.concatenate([spread[:, :, 512:1024].reshape(64, 512), out_mine], axis=0)
    second = ring_stack(second, "x")
    second = ring_stack(second, Y)
    fc_matrix, out_matrix = place_call(
        place_second, places, ring_blocks(second, "z"), [(4, 1024, 512), (512, 1024)]
    )
    third = ring_stack(proj_weight[0], "z")
    third = ring_stack(third, "x")
    proj_matrix = place_call(place_third, places, ring_blocks(third, Y), [(4, 512, 1024)])[0]

    rows_z = ring_stack(own, "z")
    group = place_call(place_rows, places, [rows_z, swap_core(rows_z)], [(2, 4, 128, 1024)])[0]
    group = group.reshape(1024, D)
    normed = layer_norm(group.astype(F32), first_gain, first_shift).astype(BF)
    projected = plain_product(normed, qkv_matrix)

    def head_columns(vector):
        parts = vector.reshape(2, 2, 2, 128)
        parts = parts.transpose(1, 0, 2, 3).reshape(8, 128)
        return lax.dynamic_index_in_dim(parts, core * 4 + z_place, 0, keepdims=False)

    q_add = head_columns(q_shift)
    v_add = head_columns(v_shift)
    zero = jnp.zeros((64,), F32)
    add = jnp.concatenate([zero, v_add[:64], zero, v_add[64:], q_add])
    projected = (projected + add).astype(BF)
    kv_msg = projected[:, :256].reshape(2, 512, 2, 128).transpose(0, 2, 1, 3)
    kv_msg = jnp.broadcast_to(kv_msg[:, :, None], (2, 2, 2, 512, 128))
    q_msg = (
        projected[:, 256:]
        .reshape(2, 4, 2, 2, 32, 2, 64)
        .transpose(0, 5, 2, 1, 4, 3, 6)
        .reshape(2, 2, 2, 128, 128)
    )
    msg = jnp.concatenate([kv_msg, q_msg], axis=3).reshape(8, 640, 128)
    got = lax.all_to_all(msg, ("yl", "x"), split_axis=0, concat_axis=0, tiled=True)

    kv, query, mix, log_total, o_msg = attend_forward(tables, got)
    o_got = lax.all_to_all(o_msg, ("yl", "x", "z"), split_axis=0, concat_axis=0, tiled=True)
    o_rows = (
        o_got.reshape(2, 2, 2, 4, 32, 2, 64).transpose(0, 2, 5, 4, 3, 1, 6).reshape(2, 128, 512)
    )
    o_two = jnp.concatenate(
        [jnp.where(core == 0, o_rows[0], o_rows[1]), jnp.where(core == 0, o_rows[1], o_rows[0])]
    )

    dm_two = jnp.concatenate([dm_own, swap_core(dm_own)], axis=0)
    part = plain_product(o_two, out_matrix)
    middle = own.astype(F32) + (part[:128] + swap_core(part[128:]) + out_shift)
    a2_own = layer_norm(middle, gain_two, shift_two).astype(BF)
    a2_two = jnp.concatenate([a2_own, swap_core(a2_own)], axis=0)

    fc_local = lax.dynamic_index_in_dim(
        fc_shift.reshape(2, 2, 1024), core, 1, keepdims=False
    ).reshape(4, 512)
    next_part = jnp.zeros((256, D), F32)
    da2_part = jnp.zeros((256, D), F32)
    dfc_list, dproj_list, dfc_shift_list = [], [], []
    for block in range(4):
        pre = plain_product(a2_two, fc_matrix[block]) + fc_local[block].astype(F32)
        act, back = jax.vjp(gelu_tanh, pre)
        act = act.astype(BF)
        next_part += plain_product(act, proj_matrix[block])
        dact = right_product(dm_two, proj_matrix[block])
        df = back(dact)[0].astype(BF)
        da2_part += right_product(df, fc_matrix[block])
        dproj_list.append(left_product(act, dm_two).astype(BF))
        dfc_list.append(left_product(a2_two, df).astype(BF))
        dfc_shift_list.append(jnp.sum(df.astype(F32), axis=0))
    final = middle + (next_part[:128] + swap_core(next_part[128:]) + proj_shift)
    da2 = da2_part[:128] + swap_core(da2_part[128:])
    back_two, normed_two = norm_backward(middle, gain_two, da2)
    dmid = dm_own.astype(F32) + back_two
    da_own = dmid.astype(BF)
    da_two = jnp.concatenate([da_own, swap_core(da_own)], axis=0)
    dout = left_product(o_two, da_two).astype(BF)
    do_two = right_product(da_two, out_matrix).astype(BF).reshape(2, 128, 512)
    do_rows = jnp.stack(
        [jnp.where(core == 0, do_two[0], do_two[1]), jnp.where(core == 0, do_two[1], do_two[0])]
    )
    do_msg = (
        do_rows.reshape(2, 2, 2, 32, 4, 2, 64).transpose(0, 5, 1, 4, 3, 2, 6).reshape(32, 32, 128)
    )
    do_got = lax.all_to_all(do_msg, ("yl", "x", "z"), split_axis=0, concat_axis=0, tiled=True)

    dproj = jnp.stack(dproj_list).reshape(4, 4, 4, 32, 1024)
    dproj = ring_reduce(dproj, Y)
    dproj = ring_reduce(dproj, "x")
    dproj = ring_reduce(dproj, "z")
    dfc = jnp.stack(dfc_list).reshape(4, 2, 2, 8, 32, 512).transpose(0, 1, 3, 2, 4, 5)
    dout_parts = (
        dout.reshape(4, 4, 2, 16, 4, 256).transpose(4, 0, 1, 3, 2, 5).reshape(4, 4, 4, 16, 512)
    )
    dsecond = jnp.concatenate([dfc.reshape(4, 4, 4, 64, 512), dout_parts], axis=3)
    dsecond = ring_reduce(dsecond, "z")
    dsecond = ring_reduce(dsecond, Y)
    dsecond = ring_reduce(dsecond, "x")

    dmsg = attend_backward(tables, (kv, query, mix, log_total), do_got)
    dgot = lax.all_to_all(dmsg, ("yl", "x"), split_axis=0, concat_axis=0, tiled=True)
    dgot = dgot.reshape(2, 2, 2, 640, 128)
    dkv = (dgot[:, :, 0, :512].astype(F32) + dgot[:, :, 1, :512].astype(F32)).astype(BF)
    dkv = dkv.transpose(0, 2, 1, 3).reshape(1024, 256)
    dq = (
        dgot[:, :, :, 512:]
        .reshape(2, 2, 2, 4, 32, 2, 64)
        .transpose(0, 3, 2, 5, 4, 1, 6)
        .reshape(1024, 128)
    )
    dqkv = jnp.concatenate([dkv, dq], axis=1)
    dqkv_matrix = left_product(normed, dqkv).astype(BF)
    da1_part = right_product(dqkv, qkv_matrix)
    group32 = group.astype(F32)
    center = group32 - jnp.mean(group32, axis=-1, keepdims=True)
    normed_one = center * lax.rsqrt(jnp.mean(center * center, axis=-1, keepdims=True) + EPS)
    dgain_one = jnp.sum(da1_part * normed_one, axis=0)
    dshift_one = jnp.sum(da1_part, axis=0)
    halves = da1_part.astype(BF).reshape(2, 4, 128, D)
    mine = lax.dynamic_index_in_dim(halves, core, 0, keepdims=False)
    other = swap_core(lax.dynamic_index_in_dim(halves, 1 - core, 0, keepdims=False))
    da1 = ring_reduce((mine.astype(F32) + other.astype(F32)).astype(BF), "z").astype(F32)
    back_one, _ = norm_backward(own.astype(F32), first_gain, da1)
    dtokens = dmid + back_one

    def spread_columns(sums):
        chunk = lax.broadcasted_iota(jnp.int32, (8, 1), 0)
        parts = jnp.where(chunk == core * 4 + z_place, sums[None, :], 0.0)
        return parts.reshape(2, 2, 2, 128).transpose(1, 0, 2, 3).reshape(1024)

    qkv_sums = jnp.sum(dqkv.astype(F32), axis=0)
    dq_shift = spread_columns(qkv_sums[256:])
    dv_shift = spread_columns(jnp.concatenate([qkv_sums[64:128], qkv_sums[192:256]]))
    dfc_shift = jnp.stack(dfc_shift_list).reshape(2, 1, 1024)
    side = lax.broadcasted_iota(jnp.int32, (1, 2, 1), 1)
    dfc_shift = jnp.where(side == core, dfc_shift, 0.0).reshape(1024, 4)
    columns = jnp.stack(
        [
            dgain_one,
            dshift_one,
            dq_shift,
            dv_shift,
            jnp.sum(da_own.astype(F32), axis=0),
            jnp.sum(da2 * normed_two, axis=0),
            jnp.sum(da2, axis=0),
            jnp.sum(dm_own.astype(F32), axis=0),
        ],
        axis=1,
    )
    columns = jnp.concatenate([columns, dfc_shift, jnp.zeros((1024, 116), F32)], axis=1)
    dfirst = jnp.concatenate([dqkv_matrix, columns.astype(BF)], axis=1)
    dfirst = dfirst.reshape(2, 2, 8, 32, 512).transpose(0, 2, 1, 3, 4).reshape(4, 4, 64, 512)
    dfirst = ring_reduce(dfirst, Y)
    dfirst = ring_reduce(dfirst, "x")

    dout_mine = dsecond[64:].reshape(16, 2, 256).transpose(1, 0, 2).reshape(1, 32, 256)
    dout_both = jnp.broadcast_to(dout_mine, (2, 32, 256)).reshape(8, 8, 256)
    back = jnp.concatenate(
        [dfirst.reshape(8, 8, 512), dsecond[:64].reshape(8, 8, 512), dout_both], axis=2
    )
    back = lax.all_to_all(back, ("core", "z"), split_axis=0, concat_axis=0, tiled=True).astype(F32)
    kv_back = back[:, :, :256].reshape(2, 2, 2, 8, 2, 2, 64).transpose(3, 5, 1, 0, 2, 4, 6)
    q_back = back[:, :, 256:384].reshape(2, 2, 2, 8, 2, 64).transpose(3, 1, 0, 2, 4, 5)
    grad_qkv = jnp.concatenate([q_back.reshape(8, 1024), kv_back.reshape(8, 2048)], axis=1)
    grad_fc = back[:, :, 512:1024].reshape(2, 2, 2, 8, 512).transpose(3, 1, 0, 2, 4).reshape(8, 4096)
    out_back = lax.dynamic_index_in_dim(
        back[:, :, 1024:].reshape(2, 4, 8, 256), core, 0, keepdims=False
    )
    grad_out = out_back.transpose(1, 0, 2).reshape(8, 1024)
    sums = jnp.sum(back[:, :, 384:396], axis=0)
    vecs = [sums[:, i][None] for i in range(8)]
    return (
        final.astype(BF)[None],
        dtokens[None],
        vecs[0],
        vecs[1],
        grad_qkv[None],
        vecs[2],
        vecs[3],
        grad_out[None],
        vecs[4],
        vecs[5],
        vecs[6],
        grad_fc[None],
        sums[:, 8:].reshape(1, 32),
        dproj.astype(F32)[None],
        vecs[7],
    )


def solution(mesh):
    fine = Mesh(mesh.devices.reshape(2, 2, 2, 4, 4), AXES)
    dp, seq, every = ("yh", "core"), ("yl", "x", "z"), AXES
    vector, matrix, tokens = P(None, every), P(None, every, None), P(dp, seq, None)
    return jax.shard_map(
        on_device,
        mesh=fine,
        in_specs=(
            tokens,
            tokens,
            P(dp, None),
            P(dp, None),
            vector,
            vector,
            matrix,
            vector,
            vector,
            matrix,
            vector,
            vector,
            vector,
            matrix,
            vector,
            matrix,
            vector,
        ),
        out_specs=(
            tokens,
            tokens,
            vector,
            vector,
            matrix,
            vector,
            vector,
            matrix,
            vector,
            vector,
            vector,
            matrix,
            vector,
            matrix,
            vector,
        ),
        check_vma=False,
    )
```

time: 4780 us -> 500 us (0.10)
  waiting for transfers between devices: 4260 us -> 145 us
  blocking collectives: 133 us -> 1.81 us
  starting transfers between devices: 0.7 us -> 112 us
  matrix products: 137 us -> 40.3 us
  local copies, waits for them, and re-layouts: 160 us -> 73.8 us
  Pallas kernels: 0 us -> 73.9 us
    reduce_scatter x4 -> x0, waiting for transfers between devices: 2550 us -> none  [the longest x1 671 us: on_device(): lax.psum_scatter(rest_sums[6], ('dp', 'seq'), scatter_dimension=0, tiled=...]
    all_gather x6 -> x0, waiting for transfers between devices: 1400 us -> none  [the longest x1 309 us: on_device(): lax.all_gather(fc_weight[layer_index], ('dp', 'seq'), axis=0, tiled=True)]
    unnamed x14 -> x0, waiting for transfers between devices: 311 us -> none
    ppermute x0 -> x62, waiting for transfers between devices: none -> 135 us  [the longest x54 135 us: shift(): return lax.ppermute(values, axis, [(i, (i + step) % 4) for i in range(4)])]
    unnamed x2 -> x1, blocking collectives: 133 us -> 1.81 us
    ppermute x0 -> x62, starting transfers between devices: none -> 81.3 us  [the longest x54 79.9 us: shift(): return lax.ppermute(values, axis, [(i, (i + step) % 4) for i in range(4)])]
    pallas_call x0 -> x6, Pallas kernels: none -> 73.9 us  [the longest x1 31.8 us: attend_backward(): pl.pallas_call(backward_kernel, out_shape=jax.ShapeDtypeStruct((8, 640, 1...]
    dot_general x64 -> x10, matrix products: 78.9 us -> 12 us  [plain_product(): return jnp.dot(left_side, right_side, preferred_element_type=F32)]
  transfers between devices with their start and end apart: 12 -> 68, of which waited for: 12 -> 27; matrix products, arithmetic and copies ran while one was open for 4% -> 23% of each run, Pallas kernels for 0% -> 15%
where the time goes in v1:
time: 500 us; the launch traced here: 493 us
  waiting for transfers between devices  145 us (29%)
  starting transfers between devices  112 us (22%)
  Pallas kernels  73.9 us (15%)
  local copies, waits for them, and re-layouts  73.8 us (15%)
  other arithmetic  42.5 us (8%)
  matrix products  40.3 us (8%)
    ppermute x54, waiting for transfers between devices, shift(): return lax.ppermute(values, axis, [(i, (i + step) % 4) for i in range(4)])  135 us
    ppermute x54, starting transfers between devices, shift(): return lax.ppermute(values, axis, [(i, (i + step) % 4) for i in range(4)])  79.9 us
    pallas_call x1, Pallas kernels, attend_backward(): pl.pallas_call(backward_kernel, out_shape=jax.ShapeDtypeStruct((8, 640, 1...  31.8 us
    pallas_call x1, Pallas kernels, attend_forward(): pl.pallas_call(forward_kernel, out_shape=shapes, in_specs=[pl.BlockSpec(m...  28.6 us
    unnamed x99, local copies, waits for them, and re-layouts  17.1 us
    dot_general x10, matrix products, left_product(): lax.dot_general(left_side, right_side, (((0,), (0,)), ((), ())), preferre...  14.6 us
    dot_general x10, matrix products, right_product(): lax.dot_general(left_side, right_side, (((1,), (1,)), ((), ())), preferre...  13.7 us
    pallas_call x4, Pallas kernels, place_call(): pl.pallas_call(kernel, out_shape=[jax.ShapeDtypeStruct(shape, BF) for sha...  13.5 us
  transfers between devices with their start and end apart: 68, of which 27 were waited for; matrix products, arithmetic and copies ran while one was open for 23% of the time, Pallas kernels for 15%

profile of v1, /device:TPU:0, one launch (start us, length us, event | category | flops | bytes accessed | tf_op | source)
XLA Modules:
  0.0 493.0 jit_solution(11356709971449076454)
XLA Ops:
  14.7 5.4 %all-to-all-start = ((bf16[8,8,1280]{2,1,0:T(8,128)(2,1)}), bf16[8,8,1280]{2,1,0:T(8,128)(2,1)S(1)}, u32[]{:S(2)}, u32[]{:S(2)}) async-start(bf16[8,8,1280]{2,1,0:T(8,128)(2,1)} %constant_dynamic-update-slice_fusion), calls=%async_computation | async-start | bytes 327680 | tf_op jit(solution)/shard_map/all_to_all | solution.py:441
  66.9 6.8 %all-to-all-start.1 = ((bf16[8,640,128]{2,1,0:T(8,128)(2,1)}), bf16[8,640,128]{2,1,0:T(8,128)(2,1)S(1)}, u32[]{:S(2)}, u32[]{:S(2)}) async-start(bf16[8,640,128]{2,1,0:T(8,128)(2,1)} %pad_maximum_fusion.2), calls=%async_computation.1 | async-start | bytes 2621440 | tf_op jit(solution)/shard_map/all_to_all | solution.py:493
  83.3 5.4 %all-to-all-done.1.got_ref = bf16[8,640,128]{2,1,0:T(8,128)(2,1)S(1)} async-done(((bf16[8,640,128]{2,1,0:T(8,128)(2,1)}), bf16[8,640,128]{2,1,0:T(8,128)(2,1)S(1)}, u32[]{:S(2)}, u32[]{:S(2)}) %all-to-all-start.1) | async-done | bytes 1310752 | tf_op jit(solution)/shard_map/all_to_all | solution.py:493
  88.7 28.6 %shard_map.282 = (bf16[4096,128]{1,0:T(8,128)(2,1)S(1)}, bf16[2048,128]{1,0:T(8,128)(2,1)S(1)}, bf16[2048,128]{1,0:T(8,128)(2,1)S(1)}, f32[8,8,256]{2,1,0:T(8,128)S(1)}, bf16[32,32,128]{2,1,0:T(8,128)(2,1)S(1)}) custom-call(s32[64]{0:T(128)S(1)} %select_reduce_fusion.order_ref, s32[32]{0:T(128)S(1)} %get-tuple-element.54.source_ref, ...), custom_call_target="tpu_custom_call" | custom-call | tf_op jit(solution)/shard_map/pallas_call | solution.py:346
  120.7 3.9 all-to-all-start.2
  130.9 6.5 %collective-permute-done.18.refs_3_ = bf16[4,4,80,512]{3,2,1,0:T(8,128)(2,1)} collective-permute-done((bf16[4,4,80,512]{3,2,1,0:T(8,128)(2,1)}, bf16[4,4,80,512]{3,2,1,0:T(8,128)(2,1)}, u32[]{:S(2)}, u32[]{:S(2)}) %collective-permute-start.18) | collective-permute-done | bytes 1310752 | tf_op jit(solution)/shard_map/ppermute | solution.py:68
  137.3 6.3 %shard_map.283 = (bf16[4,1024,512]{2,1,0:T(8,128)(2,1)}, bf16[512,1024]{1,0:T(8,128)(2,1)S(1)}) custom-call(s32[4]{0:T(128)S(1)} %pad_add_fusion.places, bf16[4,4,80,512]{3,2,1,0:T(8,128)(2,1)} %pad_maximum_fusion.3.refs_0_, bf16[4,4,80,512]{3,2,1,0:T(8,128)(2,1)} %collective-permute-done.16.refs_1_, ...), custom_call_target="tpu_custom_call" | custom-call | tf_op jit(solution)/shard_map/pallas_call | solution.py:84
  161.9 4.0 collective-permute-done.26
  165.9 6.7 %collective-permute-done.25 = bf16[4,32,1024]{2,1,0:T(8,128)(2,1)S(1)} collective-permute-done((bf16[4,32,1024]{2,1,0:T(8,128)(2,1)S(1)}, bf16[4,32,1024]{2,1,0:T(8,128)(2,1)S(1)}, u32[]{:S(2)}, u32[]{:S(2)}) %collective-permute-start.25) | collective-permute-done | bytes 262176 | tf_op jit(solution)/shard_map/ppermute | solution.py:68
  180.4 18.6 %collective-permute-done.27.refs_1_ = bf16[4,4,32,1024]{3,2,1,0:T(8,128)(2,1)} collective-permute-done((bf16[4,4,32,1024]{3,2,1,0:T(8,128)(2,1)S(1)}, bf16[4,4,32,1024]{3,2,1,0:T(8,128)(2,1)}, u32[]{:S(2)}, u32[]{:S(2)}) %collective-permute-start.27) | collective-permute-done | bytes 1048608 | tf_op jit(solution)/shard_map/ppermute | solution.py:68
  201.3 20.8 %collective-permute-done.29.refs_3_ = bf16[4,4,32,1024]{3,2,1,0:T(8,128)(2,1)} collective-permute-done((bf16[4,4,32,1024]{3,2,1,0:T(8,128)(2,1)S(1)}, bf16[4,4,32,1024]{3,2,1,0:T(8,128)(2,1)}, u32[]{:S(2)}, u32[]{:S(2)}) %collective-permute-start.29) | collective-permute-done | bytes 1048608 | tf_op jit(solution)/shard_map/ppermute | solution.py:68
  222.1 5.0 %shard_map.284 = bf16[4,512,1024]{2,1,0:T(8,128)(2,1)} custom-call(s32[4]{0:T(128)S(1)} %pad_add_fusion.places, bf16[4,4,32,1024]{3,2,1,0:T(8,128)(2,1)S(1)} %pad_maximum_fusion.5.refs_0_, bf16[4,4,32,1024]{3,2,1,0:T(8,128)(2,1)} %collective-permute-done.27.refs_1_, bf16[4,4,32,1024]{3,2,1,0:T(8,128)(2,1)} %collective-permute-done.28.refs_2_, ...), custom_call_target="tpu_custom_call" | custom-call | tf_op jit(solution)/shard_map/pallas_call | solution.py:84
  274.5 6.3 %all-to-all-start.3 = ((bf16[32,32,128]{2,1,0:T(8,128)(2,1)}), bf16[32,32,128]{2,1,0:T(8,128)(2,1)S(1)}, u32[]{:S(2)}, u32[]{:S(2)}) async-start(bf16[32,32,128]{2,1,0:T(8,128)(2,1)} %reshape.410), calls=%async_computation.3 | async-start | bytes 524288 | tf_op jit(solution)/shard_map/all_to_all | solution.py:541
  289.0 4.3 fusion.15
  298.2 20.8 %collective-permute-done.53 = bf16[4,4,32,1024]{3,2,1,0:T(8,128)(2,1)} collective-permute-done((bf16[4,4,32,1024]{3,2,1,0:T(8,128)(2,1)}, bf16[4,4,32,1024]{3,2,1,0:T(8,128)(2,1)}, u32[]{:S(2)}, u32[]{:S(2)}) %collective-permute-start.53) | collective-permute-done | bytes 1048608 | tf_op jit(solution)/shard_map/ppermute | solution.py:68
  331.0 31.8 %shard_map.285 = bf16[8,640,128]{2,1,0:T(8,128)(2,1)} custom-call(s32[64]{0:T(128)S(1)} %select_reduce_fusion.order_ref, s32[32]{0:T(128)S(1)} %get-tuple-element.54.source_ref, s32[32]{0:T(128)S(1)} %get-tuple-element.53.where_ref, s32[6]{0:T(128)S(1)} %slice_bitcast_fusion.29.starts_ref, bf16[4096,128]{1,0:T(8,128)(2,1)S(1)} %copy-done.4, ...), custom_call_target="tpu_custom_call" | custom-call | tf_op jit(solution)/shard_map/pallas_call | solution.py:357
  362.8 4.4 all-to-all-start.4
  373.8 18.4 %collective-permute-done.57 = bf16[4,32,1024]{2,1,0:T(8,128)(2,1)} collective-permute-done((bf16[4,32,1024]{2,1,0:T(8,128)(2,1)}, bf16[4,32,1024]{2,1,0:T(8,128)(2,1)}, u32[]{:S(2)}, u32[]{:S(2)}) %collective-permute-start.57) | collective-permute-done | bytes 262176 | tf_op jit(solution)/shard_map/ppermute | solution.py:68
  421.8 4.0 fusion.117
  436.1 7.2 %collective-permute-done.40 = bf16[4,64,512]{2,1,0:T(8,128)(2,1)S(1)} collective-permute-done((bf16[4,64,512]{2,1,0:T(8,128)(2,1)S(1)}, bf16[4,64,512]{2,1,0:T(8,128)(2,1)S(1)}, u32[]{:S(2)}, u32[]{:S(2)}) %collective-permute-start.40) | collective-permute-done | bytes 262176 | tf_op jit(solution)/shard_map/ppermute | solution.py:68
  458.7 4.3 all-to-all-start.5
  464.5 4.3 all-to-all-done.5
  478.4 5.5 %collective-permute-done.37 = bf16[128,1024]{1,0:T(8,128)(2,1)S(1)} collective-permute-done((bf16[128,1024]{1,0:T(8,128)(2,1)S(1)}, bf16[128,1024]{1,0:T(8,128)(2,1)S(1)}, u32[]{:S(2)}, u32[]{:S(2)}) %collective-permute-start.37) | collective-permute-done | bytes 262176 | tf_op jit(solution)/shard_map/ppermute | solution.py:68
  487.3 3.9 collective-permute-done.35
  (431 shorter events, 256.7 us)
Async XLA Ops:
  76.3 52.7 %collective-permute-start.16 = (bf16[4,4,80,512]{3,2,1,0:T(8,128)(2,1)}, bf16[4,4,80,512]{3,2,1,0:T(8,128)(2,1)}, u32[]{:S(2)}, u32[]{:S(2)}) collective-permute-start(bf16[4,4,80,512]{3,2,1,0:T(8,128)(2,1)} %pad_maximum_fusion.3.refs_0_), channel_id=1, source_target_pairs={{0,3},{1,0},{2,1},{3,2},{4,7},{5,4},{6,5},{7,6},{8,11},{9,8},{10,9... | collective-permute-start | bytes 3932168 | tf_op jit(solution)/shard_map/ppermute | solution.py:68
  78.1 52.3 %collective-permute-start.17 = (bf16[4,4,80,512]{3,2,1,0:T(8,128)(2,1)}, bf16[4,4,80,512]{3,2,1,0:T(8,128)(2,1)}, u32[]{:S(2)}, u32[]{:S(2)}) collective-permute-start(bf16[4,4,80,512]{3,2,1,0:T(8,128)(2,1)} %pad_maximum_fusion.3.refs_0_), channel_id=1, source_target_pairs={{0,2},{1,3},{2,0},{3,1},{4,6},{5,7},{6,4},{7,5},{8,10},{9,11},{10,... | collective-permute-start | bytes 3932168 | tf_op jit(solution)/shard_map/ppermute | solution.py:68
  79.2 58.2 %collective-permute-start.18 = (bf16[4,4,80,512]{3,2,1,0:T(8,128)(2,1)}, bf16[4,4,80,512]{3,2,1,0:T(8,128)(2,1)}, u32[]{:S(2)}, u32[]{:S(2)}) collective-permute-start(bf16[4,4,80,512]{3,2,1,0:T(8,128)(2,1)} %pad_maximum_fusion.3.refs_0_), channel_id=1, source_target_pairs={{0,1},{1,2},{2,3},{3,0},{4,5},{5,6},{6,7},{7,4},{8,9},{9,10},{10,1... | collective-permute-start | bytes 3932168 | tf_op jit(solution)/shard_map/ppermute | solution.py:68
  124.5 30.4 %collective-permute-start.23 = (bf16[32,1024]{1,0:T(8,128)(2,1)}, bf16[32,1024]{1,0:T(8,128)(2,1)}, u32[]{:S(2)}, u32[]{:S(2)}) collective-permute-start(bf16[32,1024]{1,0:T(8,128)(2,1)} %bitcast.405), channel_id=1, source_target_pairs={{0,1},{1,2},{2,3},{3,0},{4,5},{5,6},{6,7},{7,4},{8,9},{9,10},{10,1... | collective-permute-start | bytes 196616 | tf_op jit(solution)/shard_map/ppermute | solution.py:68
  126.3 28.7 %collective-permute-start.22 = (bf16[32,1024]{1,0:T(8,128)(2,1)}, bf16[32,1024]{1,0:T(8,128)(2,1)}, u32[]{:S(2)}, u32[]{:S(2)}) collective-permute-start(bf16[32,1024]{1,0:T(8,128)(2,1)} %bitcast.406), channel_id=1, source_target_pairs={{0,2},{1,3},{2,0},{3,1},{4,6},{5,7},{6,4},{7,5},{8,10},{9,11},{10,... | collective-permute-start | bytes 196616 | tf_op jit(solution)/shard_map/ppermute | solution.py:68
  129.0 26.0 %collective-permute-start.21 = (bf16[32,1024]{1,0:T(8,128)(2,1)}, bf16[32,1024]{1,0:T(8,128)(2,1)}, u32[]{:S(2)}, u32[]{:S(2)}) collective-permute-start(bf16[32,1024]{1,0:T(8,128)(2,1)} %bitcast.407), channel_id=1, source_target_pairs={{0,3},{1,0},{2,1},{3,2},{4,7},{5,4},{6,5},{7,6},{8,11},{9,8},{10,9... | collective-permute-start | bytes 196616 | tf_op jit(solution)/shard_map/ppermute | solution.py:68
  130.4 100.1 %collective-permute-start.31 = (bf16[128,1024]{1,0:T(8,128)(2,1)}, bf16[128,1024]{1,0:T(8,128)(2,1)}, u32[]{:S(2)}, u32[]{:S(2)}) collective-permute-start(bf16[128,1024]{1,0:T(8,128)(2,1)} %bitcast.371), channel_id=1, source_target_pairs={{0,32},{32,0},{1,33},{33,1},{2,34},{34,2},{3,35},{35,3},{4,36},{36... | collective-permute-start | bytes 786440 | tf_op jit(solution)/shard_map/ppermute | solution.py:72
  172.8 26.2 %collective-permute-start.27 = (bf16[4,4,32,1024]{3,2,1,0:T(8,128)(2,1)S(1)}, bf16[4,4,32,1024]{3,2,1,0:T(8,128)(2,1)}, u32[]{:S(2)}, u32[]{:S(2)}) collective-permute-start(bf16[4,4,32,1024]{3,2,1,0:T(8,128)(2,1)S(1)} %pad_maximum_fusion.5.refs_0_), channel_id=1, source_target_pairs={{0,80},{16,0},{64,16},{80,64},{1,81},{17,1},{65,17},{81,65},{2,82}... | collective-permute-start | bytes 3145736 | tf_op jit(solution)/shard_map/ppermute | solution.py:68
  173.6 27.7 %collective-permute-start.28 = (bf16[4,4,32,1024]{3,2,1,0:T(8,128)(2,1)S(1)}, bf16[4,4,32,1024]{3,2,1,0:T(8,128)(2,1)}, u32[]{:S(2)}, u32[]{:S(2)}) collective-permute-start(bf16[4,4,32,1024]{3,2,1,0:T(8,128)(2,1)S(1)} %pad_maximum_fusion.5.refs_0_), channel_id=1, source_target_pairs={{0,64},{16,80},{64,0},{80,16},{1,65},{17,81},{65,1},{81,17},{2,66}... | collective-permute-start | bytes 3145736 | tf_op jit(solution)/shard_map/ppermute | solution.py:68
  176.4 45.8 %collective-permute-start.29 = (bf16[4,4,32,1024]{3,2,1,0:T(8,128)(2,1)S(1)}, bf16[4,4,32,1024]{3,2,1,0:T(8,128)(2,1)}, u32[]{:S(2)}, u32[]{:S(2)}) collective-permute-start(bf16[4,4,32,1024]{3,2,1,0:T(8,128)(2,1)S(1)} %pad_maximum_fusion.5.refs_0_), channel_id=1, source_target_pairs={{0,16},{16,64},{64,80},{80,0},{1,17},{17,65},{65,81},{81,1},{2,18}... | collective-permute-start | bytes 3145736 | tf_op jit(solution)/shard_map/ppermute | solution.py:68
  178.3 48.9 %collective-permute-start.20 = (bf16[128,1024]{1,0:T(8,128)(2,1)}, bf16[128,1024]{1,0:T(8,128)(2,1)}, u32[]{:S(2)}, u32[]{:S(2)}) collective-permute-start(bf16[128,1024]{1,0:T(8,128)(2,1)} %add_convert_fusion.3), channel_id=1, source_target_pairs={{0,32},{32,0},{1,33},{33,1},{2,34},{34,2},{3,35},{35,3},{4,36},{36... | collective-permute-start | bytes 786440 | tf_op jit(solution)/shard_map/ppermute | solution.py:72
  267.5 29.8 %collective-permute-start.55 = (bf16[4,4,32,1024]{3,2,1,0:T(8,128)(2,1)}, bf16[4,4,32,1024]{3,2,1,0:T(8,128)(2,1)}, u32[]{:S(2)}, u32[]{:S(2)}) collective-permute-start(bf16[4,4,32,1024]{3,2,1,0:T(8,128)(2,1)} %get-tuple-element.66), channel_id=1, source_target_pairs={{0,80},{16,0},{64,16},{80,64},{1,81},{17,1},{65,17},{81,65},{2,82}... | collective-permute-start | bytes 3145736 | tf_op jit(solution)/shard_map/ppermute | solution.py:68
  268.2 30.0 %collective-permute-start.54 = (bf16[4,4,32,1024]{3,2,1,0:T(8,128)(2,1)}, bf16[4,4,32,1024]{3,2,1,0:T(8,128)(2,1)}, u32[]{:S(2)}, u32[]{:S(2)}) collective-permute-start(bf16[4,4,32,1024]{3,2,1,0:T(8,128)(2,1)} %get-tuple-element.67), channel_id=1, source_target_pairs={{0,64},{16,80},{64,0},{80,16},{1,65},{17,81},{65,1},{81,17},{2,66}... | collective-permute-start | bytes 3145736 | tf_op jit(solution)/shard_map/ppermute | solution.py:68
  271.0 48.1 %collective-permute-start.53 = (bf16[4,4,32,1024]{3,2,1,0:T(8,128)(2,1)}, bf16[4,4,32,1024]{3,2,1,0:T(8,128)(2,1)}, u32[]{:S(2)}, u32[]{:S(2)}) collective-permute-start(bf16[4,4,32,1024]{3,2,1,0:T(8,128)(2,1)} %get-tuple-element.65), channel_id=1, source_target_pairs={{0,16},{16,64},{64,80},{80,0},{1,17},{17,65},{65,81},{81,1},{2,18}... | collective-permute-start | bytes 3145736 | tf_op jit(solution)/shard_map/ppermute | solution.py:68
  274.5 54.4 %all-to-all-start.3 = ((bf16[32,32,128]{2,1,0:T(8,128)(2,1)}), bf16[32,32,128]{2,1,0:T(8,128)(2,1)S(1)}, u32[]{:S(2)}, u32[]{:S(2)}) async-start(bf16[32,32,128]{2,1,0:T(8,128)(2,1)} %reshape.410), calls=%async_computation.3 | async-start | bytes 524288 | tf_op jit(solution)/shard_map/all_to_all | solution.py:541
  293.3 106.7 %collective-permute-start.46 = (bf16[4,4,80,512]{3,2,1,0:T(8,128)(2,1)}, bf16[4,4,80,512]{3,2,1,0:T(8,128)(2,1)}, u32[]{:S(2)}, u32[]{:S(2)}) collective-permute-start(bf16[4,4,80,512]{3,2,1,0:T(8,128)(2,1)} %get-tuple-element.64), channel_id=1, source_target_pairs={{0,3},{1,0},{2,1},{3,2},{4,7},{5,4},{6,5},{7,6},{8,11},{9,8},{10,9... | collective-permute-start | bytes 3932168 | tf_op jit(solution)/shard_map/ppermute | solution.py:68
  296.5 103.5 %collective-permute-start.45 = (bf16[4,4,80,512]{3,2,1,0:T(8,128)(2,1)}, bf16[4,4,80,512]{3,2,1,0:T(8,128)(2,1)}, u32[]{:S(2)}, u32[]{:S(2)}) collective-permute-start(bf16[4,4,80,512]{3,2,1,0:T(8,128)(2,1)} %get-tuple-element.63), channel_id=1, source_target_pairs={{0,2},{1,3},{2,0},{3,1},{4,6},{5,7},{6,4},{7,5},{8,10},{9,11},{10,... | collective-permute-start | bytes 3932168 | tf_op jit(solution)/shard_map/ppermute | solution.py:68
  297.3 102.7 %collective-permute-start.44 = (bf16[4,4,80,512]{3,2,1,0:T(8,128)(2,1)}, bf16[4,4,80,512]{3,2,1,0:T(8,128)(2,1)}, u32[]{:S(2)}, u32[]{:S(2)}) collective-permute-start(bf16[4,4,80,512]{3,2,1,0:T(8,128)(2,1)} %get-tuple-element.62), channel_id=1, source_target_pairs={{0,1},{1,2},{2,3},{3,0},{4,5},{5,6},{6,7},{7,4},{8,9},{9,10},{10,1... | collective-permute-start | bytes 3932168 | tf_op jit(solution)/shard_map/ppermute | solution.py:68
  324.1 46.5 %collective-permute-start.58 = (bf16[4,32,1024]{2,1,0:T(8,128)(2,1)}, bf16[4,32,1024]{2,1,0:T(8,128)(2,1)}, u32[]{:S(2)}, u32[]{:S(2)}) collective-permute-start(bf16[4,32,1024]{2,1,0:T(8,128)(2,1)} %get-tuple-element.73), channel_id=1, source_target_pairs={{0,12},{4,0},{8,4},{12,8},{1,13},{5,1},{9,5},{13,9},{2,14},{6,2},{... | collective-permute-start | bytes 786440 | tf_op jit(solution)/shard_map/ppermute | solution.py:68
  362.8 46.3 %all-to-all-start.4 = ((bf16[8,640,128]{2,1,0:T(8,128)(2,1)}), bf16[8,640,128]{2,1,0:T(8,128)(2,1)}, u32[]{:S(2)}, u32[]{:S(2)}) async-start(bf16[8,640,128]{2,1,0:T(8,128)(2,1)} %shard_map.285), calls=%async_computation.4 | async-start | bytes 2621440 | tf_op jit(solution)/shard_map/all_to_all | solution.py:557
  397.3 65.7 %collective-permute-start.61 = (bf16[32,1024]{1,0:T(8,128)(2,1)}, bf16[32,1024]{1,0:T(8,128)(2,1)S(1)}, u32[]{:S(2)}, u32[]{:S(2)}) collective-permute-start(bf16[32,1024]{1,0:T(8,128)(2,1)} %get-tuple-element.90), channel_id=1, source_target_pairs={{0,3},{1,0},{2,1},{3,2},{4,7},{5,4},{6,5},{7,6},{8,11},{9,8},{10,9... | collective-permute-start | bytes 196616 | tf_op jit(solution)/shard_map/ppermute | solution.py:68
  399.4 63.6 %collective-permute-start.60 = (bf16[32,1024]{1,0:T(8,128)(2,1)}, bf16[32,1024]{1,0:T(8,128)(2,1)}, u32[]{:S(2)}, u32[]{:S(2)}) collective-permute-start(bf16[32,1024]{1,0:T(8,128)(2,1)} %get-tuple-element.91), channel_id=1, source_target_pairs={{0,2},{1,3},{2,0},{3,1},{4,6},{5,7},{6,4},{7,5},{8,10},{9,11},{10,... | collective-permute-start | bytes 196616 | tf_op jit(solution)/shard_map/ppermute | solution.py:68
  405.3 25.1 %collective-permute-start.49 = (bf16[4,80,512]{2,1,0:T(8,128)(2,1)}, bf16[4,80,512]{2,1,0:T(8,128)(2,1)}, u32[]{:S(2)}, u32[]{:S(2)}) collective-permute-start(bf16[4,80,512]{2,1,0:T(8,128)(2,1)} %get-tuple-element.70), channel_id=1, source_target_pairs={{0,80},{16,0},{64,16},{80,64},{1,81},{17,1},{65,17},{81,65},{2,82}... | collective-permute-start | bytes 983048 | tf_op jit(solution)/shard_map/ppermute | solution.py:68
  405.4 28.3 %collective-permute-start.48 = (bf16[4,80,512]{2,1,0:T(8,128)(2,1)}, bf16[4,80,512]{2,1,0:T(8,128)(2,1)}, u32[]{:S(2)}, u32[]{:S(2)}) collective-permute-start(bf16[4,80,512]{2,1,0:T(8,128)(2,1)} %get-tuple-element.71), channel_id=1, source_target_pairs={{0,64},{16,80},{64,0},{80,16},{1,65},{17,81},{65,1},{81,17},{2,66}... | collective-permute-start | bytes 983048 | tf_op jit(solution)/shard_map/ppermute | solution.py:68
  (89 other events, 969.3 us)
